TPU v7x, 32 devices: a whole 2x2x4 slice. The times are simulated.
32 devices in a mesh: rows: 8 (over z, core), cols: 4 (over y, x).
Axes of the slice: x: 2, y: 2, z: 4, core: 2. Of those that a mesh axis runs over, the one named last changes fastest.
Arguments:
- tensor: float32 [32, 1024, 512], P(None, 'rows', 'cols'), may hold values from -307200 to 307200
- second_init: float32 [512, 64], P('cols'), may hold values from -6 to 6
- third_init: float32 [32, 64], replicated, may hold values from -6 to 6
Outputs:
- first: float32 [1024, 64], P('rows')
- second: float32 [512, 64], P('cols')
- third: float32 [32, 64], replicated
All inputs are finite; a program needn't handle non-finite values.
Results may differ from a plain program's by a relative error of at most 0.0003.
Values sent between devices are 32-bit elements; how exact they have to be, the bound alone decides.
A program may use at most 64 MiB of HBM per device.

v0:
```python
import jax
import jax.numpy as jnp
from jax import lax
from jax.sharding import PartitionSpec as P

ITERS = 5


EPSILON = 1e-05
HIGHEST = lax.Precision.HIGHEST


def solve_right(rhs_rows, system):
    cholesky_low = jnp.linalg.cholesky(system)
    halfway = lax.linalg.triangular_solve(
        cholesky_low, rhs_rows, left_side=False, lower=True, transpose_a=True
    )
    return lax.linalg.triangular_solve(cholesky_low, halfway, left_side=False, lower=True)


def gram_local(factor):
    return jnp.dot(factor.T, factor, precision=HIGHEST, preferred_element_type=jnp.float32)


def settle(raw_share, total_rows):
    squares = lax.psum(jnp.sum(raw_share * raw_share, axis=0), ("rows", "cols"))
    col_scale = jnp.sqrt(squares / total_rows + EPSILON)
    normed = raw_share / col_scale
    gram_whole = lax.psum(gram_local(normed), ("rows", "cols"))
    return (col_scale, gram_whole)


def per_device(tensor, second_init, third_init):
    rows_here = tensor.shape[1]
    cols_here = tensor.shape[2]
    total_first = rows_here * lax.axis_size("rows")
    total_second = cols_here * lax.axis_size("cols")
    share_first = rows_here // lax.axis_size("cols")
    share_second = cols_here // lax.axis_size("rows")
    start_first = lax.axis_index("cols") * share_first
    start_second = lax.axis_index("rows") * share_second
    col_scale, gram_second = settle(
        lax.dynamic_slice_in_dim(second_init, start_second, share_second, 0), total_second
    )
    second = second_init / col_scale
    third = third_init
    gram_third = gram_local(third)
    first = None
    for sweep_index in range(ITERS):
        contract_first = lax.dot_general(
            second,
            tensor,
            (((0,), (2,)), ((), ())),
            precision=HIGHEST,
            preferred_element_type=jnp.float32,
        )
        system_first = gram_third * gram_second
        gram_first = None
        partial_first = jnp.einsum("rki,kr->ir", contract_first, third, precision=HIGHEST)
        mttkrp_first = lax.psum(partial_first, "cols")
        raw_block = solve_right(mttkrp_first, system_first)
        col_scale, gram_first = settle(
            lax.dynamic_slice_in_dim(raw_block, start_first, share_first, 0), total_first
        )
        carried_first = raw_block / col_scale
        contract_second = lax.dot_general(
            carried_first,
            tensor,
            (((0,), (1,)), ((), ())),
            precision=HIGHEST,
            preferred_element_type=jnp.float32,
        )
        partial_second = jnp.einsum("rkj,kr->jr", contract_second, third, precision=HIGHEST)
        outgoing = partial_second
        summed_second = lax.psum(outgoing, "rows")
        first = carried_first
        system_second = gram_third * gram_first
        raw_block = solve_right(summed_second, system_second)
        raw_part = lax.dynamic_slice_in_dim(raw_block, start_second, share_second, 0)
        col_scale, gram_second = settle(raw_part, total_second)
        carried_second = raw_block / col_scale
        partial_third = jnp.einsum("rkj,jr->kr", contract_second, carried_second, precision=HIGHEST)
        outgoing = partial_third
        summed_third = lax.psum(outgoing, ("rows", "cols"))
        second = carried_second
        third = solve_right(summed_third, gram_first * gram_second)
        gram_third = gram_local(third)
    return (first, second, third)


def solution(mesh):
    return jax.shard_map(
        per_device,
        mesh=mesh,
        in_specs=(P(None, "rows", "cols"), P("cols", None), P()),
        out_specs=(P("rows", None), P("cols", None), P()),
        check_vma=False,
    )
```

profile of v0, /device:TPU:0, one launch (start us, length us, event | category | flops | bytes accessed | tf_op | source)
XLA Modules:
  0.0 1341.7 jit_solution(9221092114014862981)
XLA Ops:
  1.7 42.0 %psum.259 = f32[64]{0:T(128)S(1)} all-reduce(f32[64]{0:T(128)S(1)} %multiply_reduce_fusion.10), channel_id=1, replica_groups=mesh['rows'=8,'cols'=4] {'rows','cols'}, use_global_device_ids=true, to_apply=%region_1.0 | all-reduce | flops 64 | bytes 512 | tf_op jit(solution)/shard_map/psum | solution.py:26
  45.7 40.3 %psum.260 = f32[64,64]{0,1:T(8,128)S(1)} all-reduce(f32[64,64]{0,1:T(8,128)S(1)} %fusion.163), channel_id=1, replica_groups=mesh['rows'=8,'cols'=4] {'rows','cols'}, use_global_device_ids=true, to_apply=%region_2.0 | all-reduce | flops 4096 | bytes 32768 | tf_op jit(solution)/shard_map/psum | solution.py:29
  104.0 17.0 %psum.261 = f32[128,64]{0,1:T(8,128)S(1)} all-reduce(f32[128,64]{0,1:T(8,128)S(1)} %bitcast.449), channel_id=1, replica_groups=mesh['rows'=8,'cols'=4] {'cols'}, use_global_device_ids=true, to_apply=%region_5.0 | all-reduce | flops 8192 | bytes 65536 | tf_op jit(solution)/shard_map/psum | solution.py:60
  121.5 38.3 %psum.262 = f32[64]{0:T(128)S(1)} all-reduce(f32[64]{0:T(128)S(1)} %multiply_reduce_fusion.9), channel_id=1, replica_groups=mesh['rows'=8,'cols'=4] {'rows','cols'}, use_global_device_ids=true, to_apply=%region_7.11 | all-reduce | flops 64 | bytes 512 | tf_op jit(solution)/shard_map/psum | solution.py:26
  160.1 40.9 %psum.263 = f32[64,64]{0,1:T(8,128)S(1)} all-reduce(f32[64,64]{0,1:T(8,128)S(1)} %fusion.160), channel_id=1, replica_groups=mesh['rows'=8,'cols'=4] {'rows','cols'}, use_global_device_ids=true, to_apply=%region_8.12 | all-reduce | flops 4096 | bytes 32768 | tf_op jit(solution)/shard_map/psum | solution.py:29
  216.0 26.7 %psum.264 = f32[128,64]{0,1:T(8,128)S(1)} all-reduce(f32[128,64]{0,1:T(8,128)S(1)} %bitcast.450), channel_id=1, replica_groups=mesh['rows'=8,'cols'=4] {'rows'}, use_global_device_ids=true, to_apply=%region_9.13 | all-reduce | flops 8192 | bytes 65536 | tf_op jit(solution)/shard_map/psum | solution.py:75
  243.3 37.8 %psum.265 = f32[64]{0:T(128)S(1)} all-reduce(f32[64]{0:T(128)S(1)} %multiply_reduce_fusion.8), channel_id=1, replica_groups=mesh['rows'=8,'cols'=4] {'rows','cols'}, use_global_device_ids=true, to_apply=%region_11.15 | all-reduce | flops 64 | bytes 512 | tf_op jit(solution)/shard_map/psum | solution.py:26
  283.6 42.9 %all-reduce.4 = (f32[32,64]{0,1:T(8,128)S(1)}, f32[64,64]{0,1:T(8,128)S(1)}) all-reduce(f32[32,64]{0,1:T(8,128)S(1)} %bitcast.444, f32[64,64]{0,1:T(8,128)S(1)} %fusion.157), channel_id=1, replica_groups=mesh['rows'=8,'cols'=4] {'rows','cols'}, use_global_device_ids=true, to_apply=%region_13.17 | all-reduce | flops 6144 | bytes 49152 | tf_op jit(solution)/shard_map/psum | solution.py:84
  355.6 16.2 %psum.268 = f32[128,64]{0,1:T(8,128)S(1)} all-reduce(f32[128,64]{0,1:T(8,128)S(1)} %bitcast.451), channel_id=1, replica_groups=mesh['rows'=8,'cols'=4] {'cols'}, use_global_device_ids=true, to_apply=%region_14.20 | all-reduce | flops 8192 | bytes 65536 | tf_op jit(solution)/shard_map/psum | solution.py:60
  372.3 37.6 %psum.269 = f32[64]{0:T(128)S(1)} all-reduce(f32[64]{0:T(128)S(1)} %multiply_reduce_fusion.7), channel_id=1, replica_groups=mesh['rows'=8,'cols'=4] {'rows','cols'}, use_global_device_ids=true, to_apply=%region_16.22 | all-reduce | flops 64 | bytes 512 | tf_op jit(solution)/shard_map/psum | solution.py:26
  410.3 41.8 %psum.270 = f32[64,64]{0,1:T(8,128)S(1)} all-reduce(f32[64,64]{0,1:T(8,128)S(1)} %fusion.155), channel_id=1, replica_groups=mesh['rows'=8,'cols'=4] {'rows','cols'}, use_global_device_ids=true, to_apply=%region_17.23 | all-reduce | flops 4096 | bytes 32768 | tf_op jit(solution)/shard_map/psum | solution.py:29
  467.1 26.0 %psum.271 = f32[128,64]{0,1:T(8,128)S(1)} all-reduce(f32[128,64]{0,1:T(8,128)S(1)} %bitcast.452), channel_id=1, replica_groups=mesh['rows'=8,'cols'=4] {'rows'}, use_global_device_ids=true, to_apply=%region_18.24 | all-reduce | flops 8192 | bytes 65536 | tf_op jit(solution)/shard_map/psum | solution.py:75
  493.7 37.7 %psum.272 = f32[64]{0:T(128)S(1)} all-reduce(f32[64]{0:T(128)S(1)} %multiply_reduce_fusion.6), channel_id=1, replica_groups=mesh['rows'=8,'cols'=4] {'rows','cols'}, use_global_device_ids=true, to_apply=%region_20.26 | all-reduce | flops 64 | bytes 512 | tf_op jit(solution)/shard_map/psum | solution.py:26
  533.9 43.0 %all-reduce.3 = (f32[32,64]{0,1:T(8,128)S(1)}, f32[64,64]{0,1:T(8,128)S(1)}) all-reduce(f32[32,64]{0,1:T(8,128)S(1)} %bitcast.445, f32[64,64]{0,1:T(8,128)S(1)} %fusion.152), channel_id=1, replica_groups=mesh['rows'=8,'cols'=4] {'rows','cols'}, use_global_device_ids=true, to_apply=%region_22.28 | all-reduce | flops 6144 | bytes 49152 | tf_op jit(solution)/shard_map/psum | solution.py:84
  606.0 16.2 %psum.275 = f32[128,64]{0,1:T(8,128)S(1)} all-reduce(f32[128,64]{0,1:T(8,128)S(1)} %bitcast.453), channel_id=1, replica_groups=mesh['rows'=8,'cols'=4] {'cols'}, use_global_device_ids=true, to_apply=%region_23.29 | all-reduce | flops 8192 | bytes 65536 | tf_op jit(solution)/shard_map/psum | solution.py:60
  622.8 37.7 %psum.276 = f32[64]{0:T(128)S(1)} all-reduce(f32[64]{0:T(128)S(1)} %multiply_reduce_fusion.5), channel_id=1, replica_groups=mesh['rows'=8,'cols'=4] {'rows','cols'}, use_global_device_ids=true, to_apply=%region_25.31 | all-reduce | flops 64 | bytes 512 | tf_op jit(solution)/shard_map/psum | solution.py:26
  660.7 42.0 %psum.277 = f32[64,64]{0,1:T(8,128)S(1)} all-reduce(f32[64,64]{0,1:T(8,128)S(1)} %fusion.150), channel_id=1, replica_groups=mesh['rows'=8,'cols'=4] {'rows','cols'}, use_global_device_ids=true, to_apply=%region_26.32 | all-reduce | flops 4096 | bytes 32768 | tf_op jit(solution)/shard_map/psum | solution.py:29
  717.7 26.0 %psum.278 = f32[128,64]{0,1:T(8,128)S(1)} all-reduce(f32[128,64]{0,1:T(8,128)S(1)} %bitcast.454), channel_id=1, replica_groups=mesh['rows'=8,'cols'=4] {'rows'}, use_global_device_ids=true, to_apply=%region_27.33 | all-reduce | flops 8192 | bytes 65536 | tf_op jit(solution)/shard_map/psum | solution.py:75
  744.3 37.8 %psum.279 = f32[64]{0:T(128)S(1)} all-reduce(f32[64]{0:T(128)S(1)} %multiply_reduce_fusion.4), channel_id=1, replica_groups=mesh['rows'=8,'cols'=4] {'rows','cols'}, use_global_device_ids=true, to_apply=%region_29.35 | all-reduce | flops 64 | bytes 512 | tf_op jit(solution)/shard_map/psum | solution.py:26
  784.6 42.8 %all-reduce.2 = (f32[32,64]{0,1:T(8,128)S(1)}, f32[64,64]{0,1:T(8,128)S(1)}) all-reduce(f32[32,64]{0,1:T(8,128)S(1)} %bitcast.446, f32[64,64]{0,1:T(8,128)S(1)} %fusion.147), channel_id=1, replica_groups=mesh['rows'=8,'cols'=4] {'rows','cols'}, use_global_device_ids=true, to_apply=%region_31.37 | all-reduce | flops 6144 | bytes 49152 | tf_op jit(solution)/shard_map/psum | solution.py:84
  856.5 16.2 %psum.282 = f32[128,64]{0,1:T(8,128)S(1)} all-reduce(f32[128,64]{0,1:T(8,128)S(1)} %bitcast.455), channel_id=1, replica_groups=mesh['rows'=8,'cols'=4] {'cols'}, use_global_device_ids=true, to_apply=%region_32.38 | all-reduce | flops 8192 | bytes 65536 | tf_op jit(solution)/shard_map/psum | solution.py:60
  873.4 37.7 %psum.283 = f32[64]{0:T(128)S(1)} all-reduce(f32[64]{0:T(128)S(1)} %multiply_reduce_fusion.3), channel_id=1, replica_groups=mesh['rows'=8,'cols'=4] {'rows','cols'}, use_global_device_ids=true, to_apply=%region_34.40 | all-reduce | flops 64 | bytes 512 | tf_op jit(solution)/shard_map/psum | solution.py:26
  911.3 41.8 %psum.284 = f32[64,64]{0,1:T(8,128)S(1)} all-reduce(f32[64,64]{0,1:T(8,128)S(1)} %fusion.145), channel_id=1, replica_groups=mesh['rows'=8,'cols'=4] {'rows','cols'}, use_global_device_ids=true, to_apply=%region_35.41 | all-reduce | flops 4096 | bytes 32768 | tf_op jit(solution)/shard_map/psum | solution.py:29
  968.0 26.0 %psum.285 = f32[128,64]{0,1:T(8,128)S(1)} all-reduce(f32[128,64]{0,1:T(8,128)S(1)} %bitcast.456), channel_id=1, replica_groups=mesh['rows'=8,'cols'=4] {'rows'}, use_global_device_ids=true, to_apply=%region_36.42 | all-reduce | flops 8192 | bytes 65536 | tf_op jit(solution)/shard_map/psum | solution.py:75
  994.7 37.8 %psum.286 = f32[64]{0:T(128)S(1)} all-reduce(f32[64]{0:T(128)S(1)} %multiply_reduce_fusion.2), channel_id=1, replica_groups=mesh['rows'=8,'cols'=4] {'rows','cols'}, use_global_device_ids=true, to_apply=%region_38.44 | all-reduce | flops 64 | bytes 512 | tf_op jit(solution)/shard_map/psum | solution.py:26
  1035.0 43.0 %all-reduce.1 = (f32[32,64]{0,1:T(8,128)S(1)}, f32[64,64]{0,1:T(8,128)S(1)}) all-reduce(f32[32,64]{0,1:T(8,128)S(1)} %bitcast.447, f32[64,64]{0,1:T(8,128)S(1)} %fusion.142), channel_id=1, replica_groups=mesh['rows'=8,'cols'=4] {'rows','cols'}, use_global_device_ids=true, to_apply=%region_40.46 | all-reduce | flops 6144 | bytes 49152 | tf_op jit(solution)/shard_map/psum | solution.py:84
  1107.1 16.3 %psum.289 = f32[128,64]{0,1:T(8,128)S(1)} all-reduce(f32[128,64]{0,1:T(8,128)S(1)} %bitcast.457), channel_id=1, replica_groups=mesh['rows'=8,'cols'=4] {'cols'}, use_global_device_ids=true, to_apply=%region_41.47 | all-reduce | flops 8192 | bytes 65536 | tf_op jit(solution)/shard_map/psum | solution.py:60
  1123.9 37.6 %psum.290 = f32[64]{0:T(128)S(1)} all-reduce(f32[64]{0:T(128)S(1)} %multiply_reduce_fusion.1), channel_id=1, replica_groups=mesh['rows'=8,'cols'=4] {'rows','cols'}, use_global_device_ids=true, to_apply=%region_43.49 | all-reduce | flops 64 | bytes 512 | tf_op jit(solution)/shard_map/psum | solution.py:26
  1162.0 41.7 %psum.291 = f32[64,64]{0,1:T(8,128)S(1)} all-reduce(f32[64,64]{0,1:T(8,128)S(1)} %fusion.140), channel_id=1, replica_groups=mesh['rows'=8,'cols'=4] {'rows','cols'}, use_global_device_ids=true, to_apply=%region_44.50 | all-reduce | flops 4096 | bytes 32768 | tf_op jit(solution)/shard_map/psum | solution.py:29
  1218.6 26.0 %psum.292 = f32[128,64]{0,1:T(8,128)S(1)} all-reduce(f32[128,64]{0,1:T(8,128)S(1)} %bitcast.458), channel_id=1, replica_groups=mesh['rows'=8,'cols'=4] {'rows'}, use_global_device_ids=true, to_apply=%region_45.51 | all-reduce | flops 8192 | bytes 65536 | tf_op jit(solution)/shard_map/psum | solution.py:75
  1245.3 37.8 %psum.293 = f32[64]{0:T(128)S(1)} all-reduce(f32[64]{0:T(128)S(1)} %multiply_reduce_fusion), channel_id=1, replica_groups=mesh['rows'=8,'cols'=4] {'rows','cols'}, use_global_device_ids=true, to_apply=%region_47.53 | all-reduce | flops 64 | bytes 512 | tf_op jit(solution)/shard_map/psum | solution.py:26
  1285.6 42.6 %all-reduce = (f32[32,64]{0,1:T(8,128)S(1)}, f32[64,64]{0,1:T(8,128)S(1)}) all-reduce(f32[32,64]{0,1:T(8,128)S(1)} %bitcast.448, f32[64,64]{0,1:T(8,128)S(1)} %fusion.138), channel_id=1, replica_groups=mesh['rows'=8,'cols'=4] {'rows','cols'}, use_global_device_ids=true, to_apply=%region_49.55 | all-reduce | flops 6144 | bytes 49152 | tf_op jit(solution)/shard_map/psum | solution.py:84
  (225 shorter events, 244.5 us)
Async XLA Ops:
  0.6 98.6 %copy-start = (f32[32,128,128]{2,1,0:T(8,128)S(1)}, f32[32,128,128]{2,1,0:T(8,128)}, u32[]{:S(2)}) copy-start(f32[32,128,128]{2,1,0:T(8,128)} %param.12) | copy-start | bytes 6291460
  1162.0 56.7 %copy-start.1 = (f32[128,64]{0,1:T(8,128)}, f32[128,64]{0,1:T(8,128)S(1)}, u32[]{:S(2)}) copy-start(f32[128,64]{0,1:T(8,128)S(1)} %broadcast_divide_fusion.1) | copy-start | bytes 98308
  1283.4 58.1 %copy-start.2 = (f32[128,64]{0,1:T(8,128)}, f32[128,64]{0,1:T(8,128)S(1)}, u32[]{:S(2)}) copy-start(f32[128,64]{0,1:T(8,128)S(1)} %broadcast_divide_fusion) | copy-start | bytes 98308
where the time goes:
time: 1350 us; the launch traced here: 1340 us
  blocking collectives  1100 us (81%)
  other arithmetic  185 us (14%)
  matrix products  57.5 us (4%)
    psum x11, blocking collectives, settle(): squares = lax.psum(jnp.sum(raw_share * raw_share, axis=0), ('rows', 'cols'))  420 us
    psum x6, blocking collectives, settle(): gram_whole = lax.psum(gram_local(normed), ('rows', 'cols'))  249 us
    psum x5, blocking collectives, per_device(): summed_third = lax.psum(outgoing, ('rows', 'cols'))  214 us
    psum x5, blocking collectives, per_device(): summed_second = lax.psum(outgoing, 'rows')  131 us
    another operation x45, other arithmetic, solve_right(): cholesky_low = jnp.linalg.cholesky(system)  97.8 us
    another operation x30, other arithmetic, solve_right(): lax.linalg.triangular_solve(cholesky_low, halfway, left_side=False, lower...  83.2 us
    psum x5, blocking collectives, per_device(): mttkrp_first = lax.psum(partial_first, 'cols')  81.8 us

commit v1 on v0

v1 whole, which is shorter than its diff:
```python
import functools

import jax
import jax.numpy as jnp
from jax import lax
from jax.experimental import pallas as pl
from jax.experimental.pallas import tpu as pltpu
from jax.sharding import PartitionSpec as P

ITERS = 5
EPSILON = 1e-05
HIGHEST = lax.Precision.HIGHEST
MESH = pl.DeviceIdType.MESH
PANEL = 8


def dot_f32(a, b):
    return jnp.dot(a, b, precision=HIGHEST, preferred_element_type=jnp.float32)


def lane_of(shape):
    return lax.broadcasted_iota(jnp.int32, shape, len(shape) - 1)


def swap_halves(x):
    return pltpu.roll(x, x.shape[1] // 2, axis=1)


def pack(x):
    n = x.shape[0] // 2
    return jnp.where(lane_of((n, x.shape[1])) < x.shape[1] // 2, x[:n], x[n:])


def unpack(x):
    other = swap_halves(x)
    left = lane_of(x.shape) < x.shape[1] // 2
    return jnp.concatenate([jnp.where(left, x, other), jnp.where(left, other, x)], axis=0)


def gram_doubled(x, rank):
    return dot_f32(x.T, x)[:rank]


def gram_scale(raw_gram, total):
    rank, wide = raw_gram.shape
    rows = lax.broadcasted_iota(jnp.int32, (rank, wide), 0)
    lanes = lane_of((rank, wide))
    diag = jnp.where((lanes == rows) | (lanes == rows + rank), raw_gram, 0.0)
    inv_row = 1.0 / jnp.sqrt(jnp.sum(diag, axis=0, keepdims=True) / total + EPSILON)
    squares_col = 0.5 * jnp.sum(diag, axis=1, keepdims=True)
    inv_col = 1.0 / jnp.sqrt(squares_col / total + EPSILON)
    return raw_gram * inv_col * inv_row, inv_row


def inverse_blocks(count, a):
    rank, wide = a.shape
    lane = lane_of((1, wide)) % rank
    sub = lax.broadcasted_iota(jnp.int32, (PANEL, wide), 0)

    def block(_, a):
        cols = [jnp.broadcast_to(a[:, q : q + 1], (rank, wide)) for q in range(PANEL)]
        for p in range(PANEL):
            here = cols[p]
            inv = 1.0 / here[p : p + 1]
            row = jnp.where(lane == p, -inv, a[p : p + 1] * inv)
            new = jnp.where(lane == p, 0.0, a) - here * row
            a = jnp.concatenate([jnp.where(sub == p, row, new[:PANEL]), new[PANEL:]], axis=0)
            for q in range(p + 1, PANEL):
                share = cols[q][p : p + 1] * inv
                new = cols[q] - here * share
                cols[q] = jnp.concatenate(
                    [jnp.where(sub == p, share, new[:PANEL]), new[PANEL:]], axis=0
                )
        a = pltpu.roll(a, wide - PANEL, axis=1)
        return jnp.concatenate([a[PANEL:], a[:PANEL]], axis=0)

    return lax.fori_loop(0, count, block, a)


def inverse(system):
    return -inverse_blocks(system.shape[0] // PANEL, system)


def solve_packed(packed, inv):
    zero = jnp.zeros_like(inv)
    top = dot_f32(packed, jnp.concatenate([inv, zero], axis=0))
    low = dot_f32(packed, jnp.concatenate([zero, inv], axis=0))
    return jnp.concatenate([top, low], axis=0)


def split_weights(x):
    high = x.astype(jnp.bfloat16).astype(jnp.float32)
    mixed = jnp.where(lane_of(x.shape) < x.shape[1] // 2, high, x - high).astype(jnp.bfloat16)
    return jnp.concatenate([mixed, mixed], axis=0)


def kernel(
    nr,
    nc,
    tensor,
    second_in,
    third_in,
    first_out,
    second_out,
    third_out,
    by_row,
    by_col,
    contracted,
    weights,
    first_d,
    second_d,
    third_d,
    gram1,
    gram2,
    gram3,
    m3_rows,
    m1_buf,
    g1_src,
    g1_buf,
    g1_all,
    m2_src,
    m2_buf,
    m2_all,
    g2_buf,
    m3_buf,
    m3_all,
    col_send,
    col_recv,
    row_send,
    row_recv,
):
    K, I, J = tensor.shape
    R = second_in.shape[1]
    my_row = lax.axis_index("rows")
    my_col = lax.axis_index("cols")

    def col_peer(d):
        return lax.rem(my_col + d, nc)

    def row_peer(d):
        return lax.rem(my_row + d, nr)

    def col_copies(kind, buf):
        return [
            pltpu.make_async_remote_copy(
                src_ref=buf.at[my_col],
                dst_ref=buf.at[my_col],
                send_sem=col_send.at[kind, d - 1],
                recv_sem=col_recv.at[kind, d - 1],
                device_id=(my_row, col_peer(d)),
                device_id_type=MESH,
            )
            for d in range(1, nc)
        ]

    def row_copies(kind, src, dst, scatter=False):
        return [
            pltpu.make_async_remote_copy(
                src_ref=src.at[row_peer(d)] if scatter else src.at[my_row],
                dst_ref=dst.at[my_row],
                send_sem=row_send.at[kind, d - 1],
                recv_sem=row_recv.at[kind, d - 1],
                device_id=(row_peer(d), my_col),
                device_id_type=MESH,
            )
            for d in range(1, nr)
        ]

    def start(copies):
        for copy in copies:
            copy.start()
        return copies

    def wait(copies):
        for copy in copies:
            copy.wait()

    def total(buf, n):
        out = buf[0]
        for s in range(1, n):
            out = out + buf[s]
        return out

    def joined(buf, n):
        return jnp.concatenate([buf[s] for s in range(n)], axis=0)

    barrier = pltpu.get_barrier_semaphore()
    for d in range(1, nc):
        pl.semaphore_signal(barrier, inc=1, device_id=(my_row, col_peer(d)), device_id_type=MESH)
    for d in range(1, nr):
        pl.semaphore_signal(barrier, inc=1, device_id=(row_peer(d), my_col), device_id_type=MESH)

    start_second = second_in[...]
    start_second = jnp.concatenate([start_second, start_second], axis=1)
    start_third = third_in[...]
    start_third = jnp.concatenate([start_third, start_third], axis=1)
    third_d[...] = start_third
    g2_buf[my_col] = pack(gram_doubled(start_second, R))
    pl.semaphore_wait(barrier, nc - 1 + nr - 1)
    copies = start(col_copies(1, g2_buf))
    gram3[...] = gram_doubled(start_third, R)

    def split_slice(k, _):
        rows = pl.ds(pl.multiple_of(k * I, I), I)
        block = tensor[k]
        high = block.astype(jnp.bfloat16)
        by_row[rows, :J] = high
        by_row[rows, J:] = (block - high.astype(jnp.float32)).astype(jnp.bfloat16)
        turned = block.T
        rows = pl.ds(pl.multiple_of(k * J, J), J)
        high = turned.astype(jnp.bfloat16)
        by_col[rows, :I] = high
        by_col[rows, I:] = (turned - high.astype(jnp.float32)).astype(jnp.bfloat16)
        return 0

    lax.fori_loop(0, K, split_slice, 0)
    wait(copies)
    gram, inv_scale = gram_scale(unpack(total(g2_buf, nc)), J * nc)
    gram2[...] = gram
    second_d[...] = start_second * inv_scale

    UNROLL = 8

    def contract(source, extent, keep):
        def step(o, acc):
            for u in range(UNROLL):
                k = o * UNROLL + u
                rows = pl.ds(pl.multiple_of(k * extent, extent), extent)
                part = jnp.dot(source[rows, :], weights[...], preferred_element_type=jnp.float32)
                if keep:
                    contracted[k] = part
                acc = acc + part * third_d[pl.ds(k, 1), :]
            return acc

        acc = lax.fori_loop(0, K // UNROLL, step, jnp.zeros((extent, 2 * R), jnp.float32))
        return acc + swap_halves(acc)

    def sweep(_, carry):
        weights[...] = split_weights(second_d[...])
        m1_buf[my_col] = pack(contract(by_row, I, False))
        m1_copies = start(col_copies(0, m1_buf))
        inv = inverse(gram3[...] * gram2[...])
        wait(m1_copies)
        raw1 = solve_packed(total(m1_buf, nc), inv)

        packed = pack(gram_doubled(raw1, R))
        share = packed.shape[0] // nc
        for c in range(nc):
            g1_src[c] = packed[c * share : (c + 1) * share]
        g1_buf[my_row] = g1_src[my_col]
        g1_copies = start(row_copies(0, g1_buf, g1_buf))
        weights[...] = split_weights(raw1)
        packed = pack(contract(by_col, J, True))
        share = packed.shape[0] // nr
        for r in range(nr):
            m2_src[r] = packed[r * share : (r + 1) * share]
        m2_buf[my_row] = m2_src[my_row]
        m2_copies = start(row_copies(1, m2_src, m2_buf, scatter=True))
        wait(g1_copies)
        g1_all[my_col] = total(g1_buf, nr)
        g1_copies = start(col_copies(2, g1_all))
        wait(m2_copies)
        m2_all[my_row] = total(m2_buf, nr)
        m2_copies = start(row_copies(2, m2_all, m2_all))
        wait(g1_copies)
        gram, scale1 = gram_scale(unpack(joined(g1_all, nc)), I * nr)
        gram1[...] = gram
        first_d[...] = raw1 * scale1

        inv = inverse(gram3[...] * gram)
        wait(m2_copies)
        raw2 = solve_packed(joined(m2_all, nr) * scale1, inv)
        g2_buf[my_col] = pack(gram_doubled(raw2, R))
        g2_copies = start(col_copies(1, g2_buf))

        scaled = raw2 * scale1
        for k in range(K):
            m3_rows[k : k + 1] = jnp.sum(contracted[k] * scaled, axis=0, keepdims=True)
        m3 = m3_rows[...]
        m3_buf[my_row] = pack(m3 + swap_halves(m3))
        m3_copies = start(row_copies(3, m3_buf, m3_buf))
        wait(g2_copies)
        gram, scale2 = gram_scale(unpack(total(g2_buf, nc)), J * nc)
        gram2[...] = gram
        second_d[...] = raw2 * scale2
        wait(m3_copies)
        m3_all[my_col] = total(m3_buf, nr)
        m3_copies = start(col_copies(3, m3_all))
        inv = inverse(gram1[...] * gram)
        wait(m3_copies)
        third = solve_packed(total(m3_all, nc) * scale2, inv)
        third_d[...] = third
        gram3[...] = gram_doubled(third, R)
        return carry

    lax.fori_loop(0, ITERS, sweep, 0)
    first_out[...] = first_d[:, :R]
    second_out[...] = second_d[:, :R]
    third_out[...] = third_d[:, :R]


def per_device(nr, nc, tensor, second_init, third_init):
    K, I, J = tensor.shape
    R = second_init.shape[1]
    wide = 2 * R
    f32 = jnp.float32
    half = R // 2

    def vmem(*shape):
        return pltpu.VMEM(shape, f32)

    return pl.pallas_call(
        functools.partial(kernel, nr, nc),
        out_shape=(
            jax.ShapeDtypeStruct((I, R), f32),
            jax.ShapeDtypeStruct((J, R), f32),
            jax.ShapeDtypeStruct((K, R), f32),
        ),
        in_specs=[pl.BlockSpec(memory_space=pltpu.VMEM)] * 3,
        out_specs=(pl.BlockSpec(memory_space=pltpu.VMEM),) * 3,
        scratch_shapes=[
            pltpu.VMEM((K * I, 2 * J), jnp.bfloat16),
            pltpu.VMEM((K * J, 2 * I), jnp.bfloat16),
            vmem(K, J, wide),
            pltpu.VMEM((2 * J, wide), jnp.bfloat16),
            vmem(I, wide),
            vmem(J, wide),
            vmem(K, wide),
            vmem(R, wide),
            vmem(R, wide),
            vmem(R, wide),
            vmem(K, wide),
            vmem(nc, I // 2, wide),
            vmem(nc, half // nc, wide),
            vmem(nr, half // nc, wide),
            vmem(nc, half // nc, wide),
            vmem(nr, J // 2 // nr, wide),
            vmem(nr, J // 2 // nr, wide),
            vmem(nr, J // 2 // nr, wide),
            vmem(nc, half, wide),
            vmem(nr, K // 2, wide),
            vmem(nc, K // 2, wide),
            pltpu.SemaphoreType.DMA((4, nc - 1)),
            pltpu.SemaphoreType.DMA((4, nc - 1)),
            pltpu.SemaphoreType.DMA((4, nr - 1)),
            pltpu.SemaphoreType.DMA((4, nr - 1)),
        ],
        compiler_params=pltpu.CompilerParams(
            collective_id=0, has_side_effects=True, vmem_limit_bytes=32 * 1024 * 1024
        ),
        cost_estimate=pl.CostEstimate(
            flops=ITERS * 2 * 2 * K * I * J * 2 * wide, bytes_accessed=4 * K * I * J, transcendentals=0
        ),
        name="als_sweeps",
    )(tensor, second_init, third_init)


def solution(mesh):
    return jax.shard_map(
        functools.partial(per_device, mesh.shape["rows"], mesh.shape["cols"]),
        mesh=mesh,
        in_specs=(P(None, "rows", "cols"), P("cols", None), P()),
        out_specs=(P("rows", None), P("cols", None), P()),
        check_vma=False,
    )
```

time: 1350 us -> 128 us (0.09)
  blocking collectives: 1100 us -> 0 us
  other arithmetic: 185 us -> 0 us
  Pallas kernels: 0 us -> 122 us
  matrix products: 57.5 us -> 0 us
    psum x32 -> x0, blocking collectives: 1100 us -> none  [the longest x11 420 us: settle(): squares = lax.psum(jnp.sum(raw_share * raw_share, axis=0), ('rows', 'cols'))]
    another operation x75 -> x0, other arithmetic: 181 us -> none  [the longest x45 97.8 us: solve_right(): cholesky_low = jnp.linalg.cholesky(system)]
    pallas_call x0 -> x1, Pallas kernels: none -> 122 us  [per_device(): pl.pallas_call(functools.partial(kernel, nr, nc), out_shape=(jax.ShapeDty...]
    dot_general x41 -> x0, matrix products: 50.6 us -> none  [the longest x5 12.7 us: per_device(): lax.dot_general(second, tensor, (((0,), (2,)), ((), ())), precision=HIGHE...]
where the time goes in v1:
time: 128 us
  Pallas kernels  122 us (95%)
  local copies, waits for them, and re-layouts  5.15 us (4%)
    pallas_call x1, Pallas kernels, per_device(): pl.pallas_call(functools.partial(kernel, nr, nc), out_shape=(jax.ShapeDty...  122 us
    unnamed x6, local copies, waits for them, and re-layouts  3.76 us

profile of v1, /device:TPU:0, one launch (start us, length us, event | category | flops | bytes accessed | tf_op | source)
XLA Modules:
  0.0 127.5 jit_solution(8446958650825975986)
XLA Ops:
  0.6 0.8 copy.6.second_in
  1.5 0.0 copy-start
  1.5 1.6 %copy-done = f32[32,128,128]{2,1,0:T(8,128)S(1)} copy-done((f32[32,128,128]{2,1,0:T(8,128)S(1)}, f32[32,128,128]{2,1,0:T(8,128)}, u32[]{:S(2)}) %copy-start) | copy-done | bytes 2097176
  3.1 0.0 copy-start.1
  3.1 0.7 copy-done.1
  3.8 121.7 %als_sweeps.1 = (f32[128,64]{1,0:T(8,128)S(1)}, f32[128,64]{1,0:T(8,128)S(1)}, f32[32,64]{1,0:T(8,128)S(1)}) custom-call(f32[32,128,128]{2,1,0:T(8,128)S(1)} %copy-done, f32[128,64]{1,0:T(8,128)S(1)} %copy.6.second_in, f32[32,64]{1,0:T(8,128)S(1)} %copy-done.1), custom_call_target="tpu_custom_call" | custom-call | flops 2684354560 | bytes 2097152 | tf_op jit(solution)/shard_map/als_sweeps/pallas_call | solution.py:312
  125.5 0.7 copy.7
  126.2 0.7 copy.8
  126.9 0.6 copy.10
Async XLA Ops:
  1.5 1.6 %copy-start = (f32[32,128,128]{2,1,0:T(8,128)S(1)}, f32[32,128,128]{2,1,0:T(8,128)}, u32[]{:S(2)}) copy-start(f32[32,128,128]{2,1,0:T(8,128)} %tensor.1) | copy-start | bytes 6291460
  3.1 0.7 copy-start.1

commit v2 on v1

--- a/solution.py
+++ b/solution.py
@@ -41,51 +41,74 @@
     return dot_f32(x.T, x)[:rank]
 
 
-def gram_scale(raw_gram, total):
-    rank, wide = raw_gram.shape
+def diag_mask(rank, wide):
     rows = lax.broadcasted_iota(jnp.int32, (rank, wide), 0)
     lanes = lane_of((rank, wide))
-    diag = jnp.where((lanes == rows) | (lanes == rows + rank), raw_gram, 0.0)
-    inv_row = 1.0 / jnp.sqrt(jnp.sum(diag, axis=0, keepdims=True) / total + EPSILON)
-    squares_col = 0.5 * jnp.sum(diag, axis=1, keepdims=True)
-    inv_col = 1.0 / jnp.sqrt(squares_col / total + EPSILON)
-    return raw_gram * inv_col * inv_row, inv_row
-
-
-def inverse_blocks(count, a):
+    return (lanes == rows) | (lanes == rows + rank)
+
+
+def col_scale(raw_gram, total):
+    diag = jnp.where(diag_mask(*raw_gram.shape), raw_gram, 0.0)
+    return jnp.sqrt(jnp.sum(diag, axis=0, keepdims=True) / total + EPSILON)
+
+
+def balance(system):
+    diag = jnp.where(diag_mask(*system.shape), system, 0.0)
+    by_lane = lax.rsqrt(jnp.sum(diag, axis=0, keepdims=True))
+    by_sub = lax.rsqrt(0.5 * jnp.sum(diag, axis=1, keepdims=True))
+    return system * by_sub * by_lane, by_lane, by_sub
+
+
+def sweep_blocks(a, first, last):
     rank, wide = a.shape
-    lane = lane_of((1, wide)) % rank
-    sub = lax.broadcasted_iota(jnp.int32, (PANEL, wide), 0)
-
-    def block(_, a):
-        cols = [jnp.broadcast_to(a[:, q : q + 1], (rank, wide)) for q in range(PANEL)]
-        for p in range(PANEL):
-            here = cols[p]
-            inv = 1.0 / here[p : p + 1]
-            row = jnp.where(lane == p, -inv, a[p : p + 1] * inv)
-            new = jnp.where(lane == p, 0.0, a) - here * row
-            a = jnp.concatenate([jnp.where(sub == p, row, new[:PANEL]), new[PANEL:]], axis=0)
-            for q in range(p + 1, PANEL):
-                share = cols[q][p : p + 1] * inv
-                new = cols[q] - here * share
-                cols[q] = jnp.concatenate(
-                    [jnp.where(sub == p, share, new[:PANEL]), new[PANEL:]], axis=0
-                )
-        a = pltpu.roll(a, wide - PANEL, axis=1)
-        return jnp.concatenate([a[PANEL:], a[:PANEL]], axis=0)
-
-    return lax.fori_loop(0, count, block, a)
-
-
-def inverse(system):
-    return -inverse_blocks(system.shape[0] // PANEL, system)
-
-
-def solve_packed(packed, inv):
+    tiles = rank // PANEL
+    tile = (PANEL, wide)
+    lane = lane_of(tile) % rank
+    sub = lax.broadcasted_iota(jnp.int32, tile, 0)
+    a = a.reshape(tiles, PANEL, wide)
+
+    for b in range(first, last):
+        base = b * PANEL
+
+        def row(x, p):
+            return jnp.broadcast_to(x[b, p : p + 1], tile)
+
+        def put(x, p, top, low):
+            mid = jnp.where(sub == p, top, jnp.where(sub == p + 1, low, x[b]))[None]
+            parts = [x[:b]] * (b > 0) + [mid] + [x[b + 1 :]] * (b + 1 < tiles)
+            return jnp.concatenate(parts, axis=0)
+
+        cols = [
+            jnp.broadcast_to(a[:, :, base + q : base + q + 1], a.shape) for q in range(PANEL)
+        ]
+        for p in range(0, PANEL, 2):
+            u, v = cols[p], cols[p + 1]
+            uu, uv, vv = row(u, p), row(u, p + 1), row(v, p + 1)
+            inv = 1.0 / (uu * vv - uv * uv)
+            iu, iv, ic = vv * inv, uu * inv, -(uv * inv)
+            for q in range(p + 2, PANEL):
+                x, y = row(cols[q], p), row(cols[q], p + 1)
+                top, low = iu * x + ic * y, ic * x + iv * y
+                cols[q] = put(cols[q] - u * top - v * low, p, top, low)
+            x, y = row(a, p), row(a, p + 1)
+            top, low = iu * x + ic * y, ic * x + iv * y
+            at_u, at_v = lane == base + p, lane == base + p + 1
+            top = jnp.where(at_u, -iu, jnp.where(at_v, -ic, top))
+            low = jnp.where(at_u, -ic, jnp.where(at_v, -iv, low))
+            kept = jnp.where((at_u | at_v)[None], 0.0, a)
+            a = put(kept - u * top - v * low, p, top, low)
+    return a.reshape(rank, wide)
+
+
+def solve_packed(packed, minus_inv):
+    wide = minus_inv.shape[1]
+    inv = -minus_inv
     zero = jnp.zeros_like(inv)
-    top = dot_f32(packed, jnp.concatenate([inv, zero], axis=0))
-    low = dot_f32(packed, jnp.concatenate([zero, inv], axis=0))
-    return jnp.concatenate([top, low], axis=0)
+    both = jnp.concatenate(
+        [jnp.concatenate([inv, zero], axis=1), jnp.concatenate([zero, inv], axis=1)], axis=0
+    )
+    out = dot_f32(packed, both)
+    return jnp.concatenate([out[:, :wide], out[:, wide:]], axis=0)
 
 
 def split_weights(x):
@@ -97,12 +120,13 @@
 def kernel(
     nr,
     nc,
-    tensor,
+    tensor_in,
     second_in,
     third_in,
     first_out,
     second_out,
     third_out,
+    tensor,
     by_row,
     by_col,
     contracted,
@@ -110,7 +134,9 @@
     first_d,
     second_d,
     third_d,
-    gram1,
+    third_raw,
+    third_inv,
+    scale2_row,
     gram2,
     gram3,
     m3_rows,
@@ -128,9 +154,10 @@
     col_recv,
     row_send,
     row_recv,
+    load_sem,
 ):
     K, I, J = tensor.shape
-    R = second_in.shape[1]
+    R = second_in.shape[0]
     my_row = lax.axis_index("rows")
     my_col = lax.axis_index("cols")
 
@@ -190,15 +217,30 @@
     for d in range(1, nr):
         pl.semaphore_signal(barrier, inc=1, device_id=(row_peer(d), my_col), device_id_type=MESH)
 
+    GROUP = 8
+    loads = [
+        pltpu.make_async_copy(
+            tensor_in.at[pl.ds(g * GROUP, GROUP)], tensor.at[pl.ds(g * GROUP, GROUP)], load_sem.at[g]
+        )
+        for g in range(K // GROUP)
+    ]
+    start(loads)
     start_second = second_in[...]
-    start_second = jnp.concatenate([start_second, start_second], axis=1)
+    start_second = jnp.concatenate([start_second, start_second], axis=0).T
     start_third = third_in[...]
     start_third = jnp.concatenate([start_third, start_third], axis=1)
-    third_d[...] = start_third
     g2_buf[my_col] = pack(gram_doubled(start_second, R))
     pl.semaphore_wait(barrier, nc - 1 + nr - 1)
     copies = start(col_copies(1, g2_buf))
-    gram3[...] = gram_doubled(start_third, R)
+
+    def settle_third(third):
+        inv_norm = 1.0 / jnp.sqrt(jnp.sum(third * third, axis=0, keepdims=True))
+        unit = third * inv_norm
+        third_d[...] = unit
+        third_inv[...] = inv_norm
+        gram3[...] = gram_doubled(unit, R)
+
+    settle_third(start_third)
 
     def split_slice(k, _):
         rows = pl.ds(pl.multiple_of(k * I, I), I)
@@ -213,35 +255,42 @@
         by_col[rows, I:] = (turned - high.astype(jnp.float32)).astype(jnp.bfloat16)
         return 0
 
-    lax.fori_loop(0, K, split_slice, 0)
+    for g, load in enumerate(loads):
+        load.wait()
+        lax.fori_loop(g * GROUP, (g + 1) * GROUP, split_slice, 0)
     wait(copies)
-    gram, inv_scale = gram_scale(unpack(total(g2_buf, nc)), J * nc)
+    gram = unpack(total(g2_buf, nc))
     gram2[...] = gram
-    second_d[...] = start_second * inv_scale
-
-    UNROLL = 8
+    scale = col_scale(gram, J * nc)
+    scale2_row[...] = scale
+    second_d[...] = start_second / scale
 
     def contract(source, extent, keep):
         def step(o, acc):
-            for u in range(UNROLL):
-                k = o * UNROLL + u
-                rows = pl.ds(pl.multiple_of(k * extent, extent), extent)
-                part = jnp.dot(source[rows, :], weights[...], preferred_element_type=jnp.float32)
+            rows = pl.ds(pl.multiple_of(o * GROUP * extent, GROUP * extent), GROUP * extent)
+            part = jnp.dot(source[rows, :], weights[...], preferred_element_type=jnp.float32)
+            for u in range(GROUP):
+                k = o * GROUP + u
+                one = part[u * extent : (u + 1) * extent]
                 if keep:
-                    contracted[k] = part
-                acc = acc + part * third_d[pl.ds(k, 1), :]
+                    contracted[k] = one
+                acc = acc + one * third_d[pl.ds(k, 1), :]
             return acc
 
-        acc = lax.fori_loop(0, K // UNROLL, step, jnp.zeros((extent, 2 * R), jnp.float32))
+        acc = lax.fori_loop(0, K // GROUP, step, jnp.zeros((extent, 2 * R), jnp.float32))
         return acc + swap_halves(acc)
+
+    BLOCKS = R // PANEL
 
     def sweep(_, carry):
         weights[...] = split_weights(second_d[...])
         m1_buf[my_col] = pack(contract(by_row, I, False))
         m1_copies = start(col_copies(0, m1_buf))
-        inv = inverse(gram3[...] * gram2[...])
+        system, by_lane, _ = balance(gram3[...] * gram2[...])
+        inv = sweep_blocks(system, 0, BLOCKS)
+        around = by_lane * scale2_row[...]
         wait(m1_copies)
-        raw1 = solve_packed(total(m1_buf, nc), inv)
+        raw1 = solve_packed(total(m1_buf, nc) * around, inv) * (around * third_inv[...])
 
         packed = pack(gram_doubled(raw1, R))
         share = packed.shape[0] // nc
@@ -263,40 +312,47 @@
         m2_all[my_row] = total(m2_buf, nr)
         m2_copies = start(row_copies(2, m2_all, m2_all))
         wait(g1_copies)
-        gram, scale1 = gram_scale(unpack(joined(g1_all, nc)), I * nr)
-        gram1[...] = gram
-        first_d[...] = raw1 * scale1
-
-        inv = inverse(gram3[...] * gram)
+
+        gram1 = unpack(joined(g1_all, nc))
+        system, by_lane1, by_sub1 = balance(gram3[...] * gram1)
+        inv = sweep_blocks(system, 0, BLOCKS)
+        gram1 = gram1 * by_sub1 * by_lane1
+        scale1 = col_scale(unpack(joined(g1_all, nc)), I * nr)
+        first_d[...] = raw1 / scale1
         wait(m2_copies)
-        raw2 = solve_packed(joined(m2_all, nr) * scale1, inv)
+        raw2 = solve_packed(joined(m2_all, nr) * by_lane1, inv) * (by_lane1 * scale1)
         g2_buf[my_col] = pack(gram_doubled(raw2, R))
         g2_copies = start(col_copies(1, g2_buf))
 
-        scaled = raw2 * scale1
+        scaled = raw2 / scale1
         for k in range(K):
             m3_rows[k : k + 1] = jnp.sum(contracted[k] * scaled, axis=0, keepdims=True)
         m3 = m3_rows[...]
         m3_buf[my_row] = pack(m3 + swap_halves(m3))
         m3_copies = start(row_copies(3, m3_buf, m3_buf))
         wait(g2_copies)
-        gram, scale2 = gram_scale(unpack(total(g2_buf, nc)), J * nc)
+        gram = unpack(total(g2_buf, nc))
         gram2[...] = gram
-        second_d[...] = raw2 * scale2
+        system, by_lane, _ = balance(gram1 * gram)
+        inv = sweep_blocks(system, 0, BLOCKS // 2)
         wait(m3_copies)
         m3_all[my_col] = total(m3_buf, nr)
         m3_copies = start(col_copies(3, m3_all))
-        inv = inverse(gram1[...] * gram)
+        inv = sweep_blocks(inv, BLOCKS // 2, BLOCKS)
+        scale2 = col_scale(gram, J * nc)
+        scale2_row[...] = scale2
+        second_d[...] = raw2 / scale2
+        around = by_lane * by_lane1 * scale1
         wait(m3_copies)
-        third = solve_packed(total(m3_all, nc) * scale2, inv)
-        third_d[...] = third
-        gram3[...] = gram_doubled(third, R)
+        third = solve_packed(total(m3_all, nc) * around, inv) * (around * scale2)
+        third_raw[...] = third
+        settle_third(third)
         return carry
 
     lax.fori_loop(0, ITERS, sweep, 0)
-    first_out[...] = first_d[:, :R]
-    second_out[...] = second_d[:, :R]
-    third_out[...] = third_d[:, :R]
+    first_out[...] = first_d[...].T[:R]
+    second_out[...] = second_d[...].T[:R]
+    third_out[...] = third_raw[:, :R]
 
 
 def per_device(nr, nc, tensor, second_init, third_init):
@@ -309,16 +365,17 @@
     def vmem(*shape):
         return pltpu.VMEM(shape, f32)
 
-    return pl.pallas_call(
+    first, second, third = pl.pallas_call(
         functools.partial(kernel, nr, nc),
         out_shape=(
-            jax.ShapeDtypeStruct((I, R), f32),
-            jax.ShapeDtypeStruct((J, R), f32),
+            jax.ShapeDtypeStruct((R, I), f32),
+            jax.ShapeDtypeStruct((R, J), f32),
             jax.ShapeDtypeStruct((K, R), f32),
         ),
-        in_specs=[pl.BlockSpec(memory_space=pltpu.VMEM)] * 3,
+        in_specs=[pl.BlockSpec(memory_space=pl.ANY)] + [pl.BlockSpec(memory_space=pltpu.VMEM)] * 2,
         out_specs=(pl.BlockSpec(memory_space=pltpu.VMEM),) * 3,
         scratch_shapes=[
+            vmem(K, I, J),
             pltpu.VMEM((K * I, 2 * J), jnp.bfloat16),
             pltpu.VMEM((K * J, 2 * I), jnp.bfloat16),
             vmem(K, J, wide),
@@ -326,7 +383,9 @@
             vmem(I, wide),
             vmem(J, wide),
             vmem(K, wide),
-            vmem(R, wide),
+            vmem(K, wide),
+            vmem(1, wide),
+            vmem(1, wide),
             vmem(R, wide),
             vmem(R, wide),
             vmem(K, wide),
@@ -344,15 +403,17 @@
             pltpu.SemaphoreType.DMA((4, nc - 1)),
             pltpu.SemaphoreType.DMA((4, nr - 1)),
             pltpu.SemaphoreType.DMA((4, nr - 1)),
+            pltpu.SemaphoreType.DMA((K // 8,)),
         ],
         compiler_params=pltpu.CompilerParams(
-            collective_id=0, has_side_effects=True, vmem_limit_bytes=32 * 1024 * 1024
+            collective_id=0, has_side_effects=True, vmem_limit_bytes=56 * 1024 * 1024
         ),
         cost_estimate=pl.CostEstimate(
             flops=ITERS * 2 * 2 * K * I * J * 2 * wide, bytes_accessed=4 * K * I * J, transcendentals=0
         ),
         name="als_sweeps",
-    )(tensor, second_init, third_init)
+    )(tensor, second_init.T, third_init)
+    return first.T, second.T, third
 
 
 def solution(mesh):

time: 128 us -> 138 us (1.078)
  Pallas kernels: 122 us -> 133 us
    pallas_call x1, Pallas kernels: 122 us -> 133 us  [per_device(): pl.pallas_call(functools.partial(kernel, nr, nc), out_shape=(jax.ShapeDty...]
    pallas_call x2 -> x0, local copies, waits for them, and re-layouts: 1.4 us -> none  [per_device(): pl.pallas_call(functools.partial(kernel, nr, nc), out_shape=(jax.ShapeDty...]
    unnamed x6 -> x3, local copies, waits for them, and re-layouts: 3.76 us -> 4.07 us
where the time goes in v2:
time: 138 us
  Pallas kernels  133 us (96%)
  local copies, waits for them, and re-layouts  4.07 us (3%)
    pallas_call x1, Pallas kernels, per_device(): pl.pallas_call(functools.partial(kernel, nr, nc), out_shape=(jax.ShapeDty...  133 us
    unnamed x3, local copies, waits for them, and re-layouts  4.07 us

profile of v2, /device:TPU:0, one launch (start us, length us, event | category | flops | bytes accessed | tf_op | source)
XLA Modules:
  0.0 137.6 jit_solution(3599786911705381063)
XLA Ops:
  0.6 132.9 %als_sweeps.1 = (f32[64,128]{1,0:T(8,128)}, f32[64,128]{1,0:T(8,128)}, f32[32,64]{1,0:T(8,128)}) custom-call(f32[32,128,128]{2,1,0:T(8,128)} %tensor_in.1, f32[64,128]{1,0:T(8,128)} %bitcast.5, f32[32,64]{1,0:T(8,128)} %third_in.1), custom_call_target="tpu_custom_call" | custom-call | flops 2684354560 | bytes 2097152 | tf_op jit(solution)/shard_map/als_sweeps/pallas_call | solution.py:368
  133.6 1.4 copy.9
  134.9 1.4 copy.10
  136.3 1.3 copy.11

commit v3 on v2

--- a/solution.py
+++ b/solution.py
@@ -59,45 +59,47 @@
     return system * by_sub * by_lane, by_lane, by_sub
 
 
-def sweep_blocks(a, first, last):
+def sweep_blocks(a, count):
     rank, wide = a.shape
     tiles = rank // PANEL
     tile = (PANEL, wide)
     lane = lane_of(tile) % rank
     sub = lax.broadcasted_iota(jnp.int32, tile, 0)
-    a = a.reshape(tiles, PANEL, wide)
-
-    for b in range(first, last):
-        base = b * PANEL
-
-        def row(x, p):
-            return jnp.broadcast_to(x[b, p : p + 1], tile)
-
-        def put(x, p, top, low):
-            mid = jnp.where(sub == p, top, jnp.where(sub == p + 1, low, x[b]))[None]
-            parts = [x[:b]] * (b > 0) + [mid] + [x[b + 1 :]] * (b + 1 < tiles)
-            return jnp.concatenate(parts, axis=0)
-
-        cols = [
-            jnp.broadcast_to(a[:, :, base + q : base + q + 1], a.shape) for q in range(PANEL)
-        ]
+
+    def row(x, p):
+        return jnp.broadcast_to(x[p : p + 1], tile)
+
+    def block(_, a):
+        head, rest = a[:PANEL], a[PANEL:].reshape(tiles - 1, PANEL, wide)
+        cols = [jnp.broadcast_to(head[:, q : q + 1], tile) for q in range(PANEL)]
         for p in range(0, PANEL, 2):
             u, v = cols[p], cols[p + 1]
             uu, uv, vv = row(u, p), row(u, p + 1), row(v, p + 1)
             inv = 1.0 / (uu * vv - uv * uv)
             iu, iv, ic = vv * inv, uu * inv, -(uv * inv)
+
+            def reduced(x):
+                x0, x1 = row(x, p), row(x, p + 1)
+                return iu * x0 + ic * x1, ic * x0 + iv * x1
+
+            def put(x, top, low):
+                new = x - u * top - v * low
+                return jnp.where(sub == p, top, jnp.where(sub == p + 1, low, new))
+
             for q in range(p + 2, PANEL):
-                x, y = row(cols[q], p), row(cols[q], p + 1)
-                top, low = iu * x + ic * y, ic * x + iv * y
-                cols[q] = put(cols[q] - u * top - v * low, p, top, low)
-            x, y = row(a, p), row(a, p + 1)
-            top, low = iu * x + ic * y, ic * x + iv * y
-            at_u, at_v = lane == base + p, lane == base + p + 1
+                cols[q] = put(cols[q], *reduced(cols[q]))
+            top, low = reduced(head)
+            at_u, at_v = lane == p, lane == p + 1
             top = jnp.where(at_u, -iu, jnp.where(at_v, -ic, top))
             low = jnp.where(at_u, -ic, jnp.where(at_v, -iv, low))
-            kept = jnp.where((at_u | at_v)[None], 0.0, a)
-            a = put(kept - u * top - v * low, p, top, low)
-    return a.reshape(rank, wide)
+            head = put(jnp.where(at_u | at_v, 0.0, head), top, low)
+        new = jnp.where((lane < PANEL)[None], 0.0, rest)
+        for q in range(PANEL):
+            new = new - jnp.broadcast_to(rest[:, :, q : q + 1], rest.shape) * row(head, q)
+        a = jnp.concatenate([new.reshape(rank - PANEL, wide), head], axis=0)
+        return pltpu.roll(a, wide - PANEL, axis=1)
+
+    return lax.fori_loop(0, count, block, a)
 
 
 def solve_packed(packed, minus_inv):
@@ -287,7 +289,7 @@
         m1_buf[my_col] = pack(contract(by_row, I, False))
         m1_copies = start(col_copies(0, m1_buf))
         system, by_lane, _ = balance(gram3[...] * gram2[...])
-        inv = sweep_blocks(system, 0, BLOCKS)
+        inv = sweep_blocks(system, BLOCKS)
         around = by_lane * scale2_row[...]
         wait(m1_copies)
         raw1 = solve_packed(total(m1_buf, nc) * around, inv) * (around * third_inv[...])
@@ -315,7 +317,7 @@
 
         gram1 = unpack(joined(g1_all, nc))
         system, by_lane1, by_sub1 = balance(gram3[...] * gram1)
-        inv = sweep_blocks(system, 0, BLOCKS)
+        inv = sweep_blocks(system, BLOCKS)
         gram1 = gram1 * by_sub1 * by_lane1
         scale1 = col_scale(unpack(joined(g1_all, nc)), I * nr)
         first_d[...] = raw1 / scale1
@@ -334,11 +336,11 @@
         gram = unpack(total(g2_buf, nc))
         gram2[...] = gram
         system, by_lane, _ = balance(gram1 * gram)
-        inv = sweep_blocks(system, 0, BLOCKS // 2)
+        inv = sweep_blocks(system, BLOCKS // 2)
         wait(m3_copies)
         m3_all[my_col] = total(m3_buf, nr)
         m3_copies = start(col_copies(3, m3_all))
-        inv = sweep_blocks(inv, BLOCKS // 2, BLOCKS)
+        inv = sweep_blocks(inv, BLOCKS - BLOCKS // 2)
         scale2 = col_scale(gram, J * nc)
         scale2_row[...] = scale2
         second_d[...] = raw2 / scale2
@@ -350,8 +352,8 @@
         return carry
 
     lax.fori_loop(0, ITERS, sweep, 0)
-    first_out[...] = first_d[...].T[:R]
-    second_out[...] = second_d[...].T[:R]
+    first_out[...] = first_d[:, :R]
+    second_out[...] = second_d[:, :R]
     third_out[...] = third_raw[:, :R]
 
 
@@ -365,11 +367,11 @@
     def vmem(*shape):
         return pltpu.VMEM(shape, f32)
 
-    first, second, third = pl.pallas_call(
+    return pl.pallas_call(
         functools.partial(kernel, nr, nc),
         out_shape=(
-            jax.ShapeDtypeStruct((R, I), f32),
-            jax.ShapeDtypeStruct((R, J), f32),
+            jax.ShapeDtypeStruct((I, R), f32),
+            jax.ShapeDtypeStruct((J, R), f32),
             jax.ShapeDtypeStruct((K, R), f32),
         ),
         in_specs=[pl.BlockSpec(memory_space=pl.ANY)] + [pl.BlockSpec(memory_space=pltpu.VMEM)] * 2,
@@ -413,7 +415,6 @@
         ),
         name="als_sweeps",
     )(tensor, second_init.T, third_init)
-    return first.T, second.T, third
 
 
 def solution(mesh):

time: 138 us -> 133 us (0.964)
  Pallas kernels: 133 us -> 128 us
    pallas_call x1, Pallas kernels: 133 us -> 128 us  [per_device(): pl.pallas_call(functools.partial(kernel, nr, nc), out_shape=(jax.ShapeDty...]
    pallas_call x0 -> x2, local copies, waits for them, and re-layouts: none -> 3.07 us  [per_device(): pl.pallas_call(functools.partial(kernel, nr, nc), out_shape=(jax.ShapeDty...]
    unnamed x3 -> x1, local copies, waits for them, and re-layouts: 4.07 us -> 1.32 us
where the time goes in v3:
time: 133 us
  Pallas kernels  128 us (96%)
  local copies, waits for them, and re-layouts  4.4 us (3%)
    pallas_call x1, Pallas kernels, per_device(): pl.pallas_call(functools.partial(kernel, nr, nc), out_shape=(jax.ShapeDty...  128 us
    pallas_call x2, local copies, waits for them, and re-layouts, per_device(): pl.pallas_call(functools.partial(kernel, nr, nc), out_shape=(jax.ShapeDty...  3.07 us

profile of v3, /device:TPU:0, one launch (start us, length us, event | category | flops | bytes accessed | tf_op | source)
XLA Modules:
  0.0 133.0 jit_solution(9678244799302636199)
XLA Ops:
  0.6 127.9 %als_sweeps.1 = (f32[128,64]{1,0:T(8,128)}, f32[128,64]{1,0:T(8,128)}, f32[32,64]{1,0:T(8,128)}) custom-call(f32[32,128,128]{2,1,0:T(8,128)} %tensor_in.1, f32[64,128]{1,0:T(8,128)} %bitcast.1, f32[32,64]{1,0:T(8,128)} %third_in.1), custom_call_target="tpu_custom_call" | custom-call | flops 2684354560 | bytes 2097152 | tf_op jit(solution)/shard_map/als_sweeps/pallas_call | solution.py:370
  128.6 1.5 %copy.6 = f32[128,64]{0,1:T(8,128)} copy(f32[128,64]{1,0:T(8,128)} %get-tuple-element.3) | data formatting | bytes 65536 | tf_op jit(solution)/shard_map/als_sweeps/pallas_call | solution.py:370
  130.1 1.5 %copy.7 = f32[128,64]{0,1:T(8,128)} copy(f32[128,64]{1,0:T(8,128)} %get-tuple-element.4) | data formatting | bytes 65536 | tf_op jit(solution)/shard_map/als_sweeps/pallas_call | solution.py:370
  131.6 1.3 copy.9

commit v4 on v3

--- a/solution.py
+++ b/solution.py
@@ -9,13 +9,8 @@
 
 ITERS = 5
 EPSILON = 1e-05
-HIGHEST = lax.Precision.HIGHEST
 MESH = pl.DeviceIdType.MESH
 PANEL = 8
-
-
-def dot_f32(a, b):
-    return jnp.dot(a, b, precision=HIGHEST, preferred_element_type=jnp.float32)
 
 
 def lane_of(shape):
@@ -37,8 +32,20 @@
     return jnp.concatenate([jnp.where(left, x, other), jnp.where(left, other, x)], axis=0)
 
 
+def split_halves(x):
+    high = x.astype(jnp.bfloat16).astype(jnp.float32)
+    return jnp.where(lane_of(x.shape) < x.shape[1] // 2, high, x - high).astype(jnp.bfloat16)
+
+
 def gram_doubled(x, rank):
-    return dot_f32(x.T, x)[:rank]
+    left = split_halves(x)
+    high = x.T.astype(jnp.bfloat16).astype(jnp.float32)
+    parts = x.T - high
+    rows = lax.broadcasted_iota(jnp.int32, parts.shape, 0)
+    turned = jnp.where(rows < rank, high, parts).astype(jnp.bfloat16)
+    all_four = jnp.dot(turned, left, preferred_element_type=jnp.float32)
+    both = all_four[:rank] + all_four[rank:]
+    return both + swap_halves(both)
 
 
 def diag_mask(rank, wide):
@@ -103,32 +110,26 @@
 
 
 def solve_packed(packed, minus_inv):
-    wide = minus_inv.shape[1]
-    inv = -minus_inv
-    zero = jnp.zeros_like(inv)
-    both = jnp.concatenate(
-        [jnp.concatenate([inv, zero], axis=1), jnp.concatenate([zero, inv], axis=1)], axis=0
-    )
-    out = dot_f32(packed, both)
-    return jnp.concatenate([out[:, :wide], out[:, wide:]], axis=0)
+    parts = split_halves(-minus_inv)
+    weights = jnp.concatenate([parts, parts], axis=0)
+    out = jnp.dot(split_halves(unpack(packed)), weights, preferred_element_type=jnp.float32)
+    return out + swap_halves(out)
 
 
 def split_weights(x):
-    high = x.astype(jnp.bfloat16).astype(jnp.float32)
-    mixed = jnp.where(lane_of(x.shape) < x.shape[1] // 2, high, x - high).astype(jnp.bfloat16)
+    mixed = split_halves(x)
     return jnp.concatenate([mixed, mixed], axis=0)
 
 
 def kernel(
     nr,
     nc,
-    tensor_in,
+    tensor,
     second_in,
     third_in,
     first_out,
     second_out,
     third_out,
-    tensor,
     by_row,
     by_col,
     contracted,
@@ -156,7 +157,6 @@
     col_recv,
     row_send,
     row_recv,
-    load_sem,
 ):
     K, I, J = tensor.shape
     R = second_in.shape[0]
@@ -220,13 +220,6 @@
         pl.semaphore_signal(barrier, inc=1, device_id=(row_peer(d), my_col), device_id_type=MESH)
 
     GROUP = 8
-    loads = [
-        pltpu.make_async_copy(
-            tensor_in.at[pl.ds(g * GROUP, GROUP)], tensor.at[pl.ds(g * GROUP, GROUP)], load_sem.at[g]
-        )
-        for g in range(K // GROUP)
-    ]
-    start(loads)
     start_second = second_in[...]
     start_second = jnp.concatenate([start_second, start_second], axis=0).T
     start_third = third_in[...]
@@ -257,9 +250,7 @@
         by_col[rows, I:] = (turned - high.astype(jnp.float32)).astype(jnp.bfloat16)
         return 0
 
-    for g, load in enumerate(loads):
-        load.wait()
-        lax.fori_loop(g * GROUP, (g + 1) * GROUP, split_slice, 0)
+    lax.fori_loop(0, K, split_slice, 0)
     wait(copies)
     gram = unpack(total(g2_buf, nc))
     gram2[...] = gram
@@ -374,10 +365,9 @@
             jax.ShapeDtypeStruct((J, R), f32),
             jax.ShapeDtypeStruct((K, R), f32),
         ),
-        in_specs=[pl.BlockSpec(memory_space=pl.ANY)] + [pl.BlockSpec(memory_space=pltpu.VMEM)] * 2,
+        in_specs=[pl.BlockSpec(memory_space=pltpu.VMEM)] * 3,
         out_specs=(pl.BlockSpec(memory_space=pltpu.VMEM),) * 3,
         scratch_shapes=[
-            vmem(K, I, J),
             pltpu.VMEM((K * I, 2 * J), jnp.bfloat16),
             pltpu.VMEM((K * J, 2 * I), jnp.bfloat16),
             vmem(K, J, wide),
@@ -405,10 +395,9 @@
             pltpu.SemaphoreType.DMA((4, nc - 1)),
             pltpu.SemaphoreType.DMA((4, nr - 1)),
             pltpu.SemaphoreType.DMA((4, nr - 1)),
-            pltpu.SemaphoreType.DMA((K // 8,)),
         ],
         compiler_params=pltpu.CompilerParams(
-            collective_id=0, has_side_effects=True, vmem_limit_bytes=56 * 1024 * 1024
+            collective_id=0, has_side_effects=True, vmem_limit_bytes=32 * 1024 * 1024
         ),
         cost_estimate=pl.CostEstimate(
             flops=ITERS * 2 * 2 * K * I * J * 2 * wide, bytes_accessed=4 * K * I * J, transcendentals=0

time: 133 us -> 133 us (level)
    unnamed x1 -> x7, local copies, waits for them, and re-layouts: 1.32 us -> 3.66 us
    pallas_call x2, local copies, waits for them, and re-layouts: 3.07 us -> 1.4 us  [per_device(): pl.pallas_call(functools.partial(kernel, nr, nc), out_shape=(jax.ShapeDty...]
where the time goes in v4:
time: 133 us
  Pallas kernels  127 us (95%)
  local copies, waits for them, and re-layouts  5.06 us (4%)
    pallas_call x1, Pallas kernels, per_device(): pl.pallas_call(functools.partial(kernel, nr, nc), out_shape=(jax.ShapeDty...  127 us
    unnamed x7, local copies, waits for them, and re-layouts  3.66 us

profile of v4, /device:TPU:0, one launch (start us, length us, event | category | flops | bytes accessed | tf_op | source)
XLA Modules:
  0.0 132.8 jit_solution(8809237235229031061)
XLA Ops:
  0.6 0.0 copy-start
  0.6 1.6 %copy-done = f32[32,128,128]{2,1,0:T(8,128)S(1)} copy-done((f32[32,128,128]{2,1,0:T(8,128)S(1)}, f32[32,128,128]{2,1,0:T(8,128)}, u32[]{:S(2)}) %copy-start) | copy-done | bytes 2097176
  2.2 0.0 copy-start.1
  2.2 0.8 copy-done.1
  3.0 0.0 copy-start.2
  3.0 0.7 copy-done.2
  3.7 127.1 %als_sweeps.1 = (f32[128,64]{1,0:T(8,128)S(1)}, f32[128,64]{1,0:T(8,128)S(1)}, f32[32,64]{1,0:T(8,128)S(1)}) custom-call(f32[32,128,128]{2,1,0:T(8,128)S(1)} %copy-done, f32[64,128]{1,0:T(8,128)S(1)} %bitcast.1, f32[32,64]{1,0:T(8,128)S(1)} %copy-done.2), custom_call_target="tpu_custom_call" | custom-call | flops 2684354560 | bytes 2097152 | tf_op jit(solution)/shard_map/als_sweeps/pallas_call | solution.py:361
  130.8 0.7 copy.6
  131.5 0.7 copy.7
  132.2 0.6 copy.9
Async XLA Ops:
  0.6 1.6 %copy-start = (f32[32,128,128]{2,1,0:T(8,128)S(1)}, f32[32,128,128]{2,1,0:T(8,128)}, u32[]{:S(2)}) copy-start(f32[32,128,128]{2,1,0:T(8,128)} %tensor.1) | copy-start | bytes 6291460
  2.2 0.8 copy-start.1
  3.0 0.7 copy-start.2

commit v5 on v4

--- a/solution.py
+++ b/solution.py
@@ -260,14 +260,13 @@
 
     def contract(source, extent, keep):
         def step(o, acc):
-            rows = pl.ds(pl.multiple_of(o * GROUP * extent, GROUP * extent), GROUP * extent)
-            part = jnp.dot(source[rows, :], weights[...], preferred_element_type=jnp.float32)
             for u in range(GROUP):
                 k = o * GROUP + u
-                one = part[u * extent : (u + 1) * extent]
+                rows = pl.ds(pl.multiple_of(k * extent, extent), extent)
+                part = jnp.dot(source[rows, :], weights[...], preferred_element_type=jnp.float32)
                 if keep:
-                    contracted[k] = one
-                acc = acc + one * third_d[pl.ds(k, 1), :]
+                    contracted[k] = part
+                acc = acc + part * third_d[pl.ds(k, 1), :]
             return acc
 
         acc = lax.fori_loop(0, K // GROUP, step, jnp.zeros((extent, 2 * R), jnp.float32))
@@ -311,13 +310,14 @@
         inv = sweep_blocks(system, BLOCKS)
         gram1 = gram1 * by_sub1 * by_lane1
         scale1 = col_scale(unpack(joined(g1_all, nc)), I * nr)
-        first_d[...] = raw1 / scale1
+        inv_scale1 = 1.0 / scale1
+        first_d[...] = raw1 * inv_scale1
         wait(m2_copies)
         raw2 = solve_packed(joined(m2_all, nr) * by_lane1, inv) * (by_lane1 * scale1)
         g2_buf[my_col] = pack(gram_doubled(raw2, R))
         g2_copies = start(col_copies(1, g2_buf))
 
-        scaled = raw2 / scale1
+        scaled = raw2 * inv_scale1
         for k in range(K):
             m3_rows[k : k + 1] = jnp.sum(contracted[k] * scaled, axis=0, keepdims=True)
         m3 = m3_rows[...]
@@ -334,7 +334,7 @@
         inv = sweep_blocks(inv, BLOCKS - BLOCKS // 2)
         scale2 = col_scale(gram, J * nc)
         scale2_row[...] = scale2
-        second_d[...] = raw2 / scale2
+        second_d[...] = raw2 * (1.0 / scale2)
         around = by_lane * by_lane1 * scale1
         wait(m3_copies)
         third = solve_packed(total(m3_all, nc) * around, inv) * (around * scale2)

time: 133 us -> 133 us (level)
  no operation moved by 1% of the time
where the time goes in v5:
time: 133 us; the launch traced here: 132 us
  Pallas kernels  127 us (95%)
  local copies, waits for them, and re-layouts  5.06 us (4%)
    pallas_call x1, Pallas kernels, per_device(): pl.pallas_call(functools.partial(kernel, nr, nc), out_shape=(jax.ShapeDty...  127 us
    unnamed x7, local copies, waits for them, and re-layouts  3.66 us

profile of v5, /device:TPU:0, one launch (start us, length us, event | category | flops | bytes accessed | tf_op | source)
XLA Modules:
  0.0 132.5 jit_solution(14152384821673571171)
XLA Ops:
  0.6 0.0 copy-start
  0.6 1.6 %copy-done = f32[32,128,128]{2,1,0:T(8,128)S(1)} copy-done((f32[32,128,128]{2,1,0:T(8,128)S(1)}, f32[32,128,128]{2,1,0:T(8,128)}, u32[]{:S(2)}) %copy-start) | copy-done | bytes 2097176
  2.2 0.0 copy-start.1
  2.2 0.8 copy-done.1
  3.0 0.0 copy-start.2
  3.0 0.7 copy-done.2
  3.7 126.8 %als_sweeps.1 = (f32[128,64]{1,0:T(8,128)S(1)}, f32[128,64]{1,0:T(8,128)S(1)}, f32[32,64]{1,0:T(8,128)S(1)}) custom-call(f32[32,128,128]{2,1,0:T(8,128)S(1)} %copy-done, f32[64,128]{1,0:T(8,128)S(1)} %bitcast.1, f32[32,64]{1,0:T(8,128)S(1)} %copy-done.2), custom_call_target="tpu_custom_call" | custom-call | flops 2684354560 | bytes 2097152 | tf_op jit(solution)/shard_map/als_sweeps/pallas_call | solution.py:361
  130.5 0.7 copy.6
  131.2 0.7 copy.7
  131.9 0.6 copy.9
Async XLA Ops:
  0.6 1.6 %copy-start = (f32[32,128,128]{2,1,0:T(8,128)S(1)}, f32[32,128,128]{2,1,0:T(8,128)}, u32[]{:S(2)}) copy-start(f32[32,128,128]{2,1,0:T(8,128)} %tensor.1) | copy-start | bytes 6291460
  2.2 0.8 copy-start.1
  3.0 0.7 copy-start.2

commit v6 on v5

--- a/solution.py
+++ b/solution.py
@@ -327,11 +327,10 @@
         gram = unpack(total(g2_buf, nc))
         gram2[...] = gram
         system, by_lane, _ = balance(gram1 * gram)
-        inv = sweep_blocks(system, BLOCKS // 2)
         wait(m3_copies)
         m3_all[my_col] = total(m3_buf, nr)
         m3_copies = start(col_copies(3, m3_all))
-        inv = sweep_blocks(inv, BLOCKS - BLOCKS // 2)
+        inv = sweep_blocks(system, BLOCKS)
         scale2 = col_scale(gram, J * nc)
         scale2_row[...] = scale2
         second_d[...] = raw2 * (1.0 / scale2)

time: 133 us -> 129 us (0.970)
  Pallas kernels: 127 us -> 123 us
    pallas_call x1, Pallas kernels: 127 us -> 123 us  [per_device(): pl.pallas_call(functools.partial(kernel, nr, nc), out_shape=(jax.ShapeDty...]
where the time goes in v6:
time: 129 us
  Pallas kernels  123 us (95%)
  local copies, waits for them, and re-layouts  5.06 us (4%)
    pallas_call x1, Pallas kernels, per_device(): pl.pallas_call(functools.partial(kernel, nr, nc), out_shape=(jax.ShapeDty...  123 us
    unnamed x7, local copies, waits for them, and re-layouts  3.66 us

profile of v6, /device:TPU:0, one launch (start us, length us, event | category | flops | bytes accessed | tf_op | source)
XLA Modules:
  0.0 128.8 jit_solution(16050062032496092425)
XLA Ops:
  0.6 0.0 copy-start
  0.6 1.6 %copy-done = f32[32,128,128]{2,1,0:T(8,128)S(1)} copy-done((f32[32,128,128]{2,1,0:T(8,128)S(1)}, f32[32,128,128]{2,1,0:T(8,128)}, u32[]{:S(2)}) %copy-start) | copy-done | bytes 2097176
  2.2 0.0 copy-start.1
  2.2 0.8 copy-done.1
  3.0 0.0 copy-start.2
  3.0 0.7 copy-done.2
  3.7 123.1 %als_sweeps.1 = (f32[128,64]{1,0:T(8,128)S(1)}, f32[128,64]{1,0:T(8,128)S(1)}, f32[32,64]{1,0:T(8,128)S(1)}) custom-call(f32[32,128,128]{2,1,0:T(8,128)S(1)} %copy-done, f32[64,128]{1,0:T(8,128)S(1)} %bitcast.1, f32[32,64]{1,0:T(8,128)S(1)} %copy-done.2), custom_call_target="tpu_custom_call" | custom-call | flops 2684354560 | bytes 2097152 | tf_op jit(solution)/shard_map/als_sweeps/pallas_call | solution.py:360
  126.8 0.7 copy.6
  127.5 0.7 copy.7
  128.2 0.6 copy.9
Async XLA Ops:
  0.6 1.6 %copy-start = (f32[32,128,128]{2,1,0:T(8,128)S(1)}, f32[32,128,128]{2,1,0:T(8,128)}, u32[]{:S(2)}) copy-start(f32[32,128,128]{2,1,0:T(8,128)} %tensor.1) | copy-start | bytes 6291460
  2.2 0.8 copy-start.1
  3.0 0.7 copy-start.2
